TPU v7x, 512 devices: a whole 4x8x8 slice. The times are simulated.
512 devices in a mesh: pool: 8 (over y), seq: 16 (over z, core), head: 4 (over x).
Axes of the slice: x: 4, y: 8, z: 8, core: 2. Of those that a mesh axis runs over, the one named last changes fastest.
Arguments:
- latents: bfloat16 [16384, 2048], P(('pool', 'seq'), 'head'), may hold values from -6 to 6
- route: int32 [16384], P(('pool', 'seq')), may hold values from 0 to 16383, as said below
- seg_lengths: int32 [8, 8], P('pool'), may hold values from 1 to 1024, 2048 in all within a row
- modulation: float32 [8, 8, 6144], P('pool'), may hold values from -3 to 3
- qkv_weight: bfloat16 [2048, 3, 1024], P(None, None, 'head'), may hold values from -0.125 to 0.125
- qk_gain: float32 [2, 64], replicated, may hold values from 0.5 to 16
- out_weight: bfloat16 [1024, 2048], P('head'), may hold values from -0.1875 to 0.1875
Outputs:
- blended: bfloat16 [16384, 2048], P(('pool', 'seq'), 'head')
Inputs may be any that keep to these rules, and one draw needn't show every extreme that they name: route is a permutation of the packed positions; position p lies on device p // 128 of pool+seq (pool slowest) at row p % 128. Of the 128 rows of one device at most 2 have positions on any one device, and some device sends exactly 2 to some device.
All inputs are finite; a program needn't handle non-finite values.
Results may differ from a plain program's by a relative error of at most 0.014.
The roundings to bfloat16 on the way count: a program that leaves them out, or rounds other values in their place, can miss the bound.
Values may be sent and summed in bfloat16 or wider, within the bound.
A program may use at most 64 MiB of HBM per device.

v0:
```python
import math

import jax
import jax.numpy as jnp
from jax import lax
from jax.sharding import PartitionSpec as P

HEAD_DIM = 64


eps_norm = 1e-06
masked_score = -1e30


def segment_of(positions, lengths):
    ends = jnp.cumsum(lengths)
    return jnp.sum((positions[:, None] >= ends[None, :]).astype(jnp.int32), axis=1)


def rms_scaled(values, gain):
    mean_sq = jnp.mean(values * values, axis=-1, keepdims=True)
    return (values * lax.rsqrt(mean_sq + eps_norm) * gain).astype(jnp.bfloat16)


def local(latents, route, seg_lengths, modulation, qkv_weight, qk_gain, out_weight):
    rows, cols = latents.shape
    n_pool = lax.axis_size("pool")
    n_seq = lax.axis_size("seq")
    peers = n_pool * n_seq
    cap = 2 * rows // peers
    target = route // rows
    slot = route % rows
    onehot = (target[:, None] == jnp.arange(peers)[None, :]).astype(jnp.int32)
    rank = jnp.sum(onehot * jnp.cumsum(onehot, axis=0), axis=1) - 1
    place = target * cap + rank
    send_rows = jnp.zeros((peers * cap, cols), jnp.bfloat16).at[place].set(latents)
    send_slot = jnp.full((peers * cap,), -1, jnp.int32).at[place].set(slot)
    got_rows, got_slot = (
        lax.all_to_all(send_rows, ("pool", "seq"), split_axis=0, concat_axis=0, tiled=True),
        lax.all_to_all(send_slot, ("pool", "seq"), split_axis=0, concat_axis=0, tiled=True),
    )
    landing = jnp.where(got_slot >= 0, got_slot, rows)
    packed = jnp.zeros((rows, cols), jnp.bfloat16).at[landing].set(got_rows, mode="drop")
    whole = lax.all_gather(packed, "head", axis=1, tiled=True)
    width = whole.shape[1]
    lengths = seg_lengths[0]
    segments = lengths.shape[0]
    seq_index = lax.axis_index("seq")
    positions = seq_index * rows + jnp.arange(rows)
    seg_query = segment_of(positions, lengths)
    pick = (seg_query[:, None] == jnp.arange(segments)[None, :]).astype(jnp.float32)
    factors = jnp.dot(pick, modulation[0], precision=lax.Precision.HIGHEST)
    shift = factors[:, :width]
    scale = factors[:, width : 2 * width]
    head_index = lax.axis_index("head")
    gate = lax.dynamic_slice_in_dim(factors, 2 * width + head_index * cols, cols, 1)
    feats = whole.astype(jnp.float32)
    centred = feats - jnp.mean(feats, axis=1, keepdims=True)
    var = jnp.mean(centred * centred, axis=1, keepdims=True)
    normed = (centred * lax.rsqrt(var + eps_norm) * (1.0 + scale) + shift).astype(jnp.bfloat16)
    projected = jnp.einsum("td,dcf->tcf", normed, qkv_weight, preferred_element_type=jnp.float32)
    local_heads = qkv_weight.shape[2] // HEAD_DIM
    query = rms_scaled(projected[:, 0].reshape(rows, local_heads, HEAD_DIM), qk_gain[0])
    keys = rms_scaled(projected[:, 1].reshape(rows, local_heads, HEAD_DIM), qk_gain[1])
    values = projected[:, 2].reshape(rows, local_heads, HEAD_DIM).astype(jnp.bfloat16)
    score_scale = 1.0 / math.sqrt(HEAD_DIM)

    def attend(carry, block):
        key_block, value_block, key_seg = block
        run_max, run_sum, run_acc = carry
        scores = (
            jnp.einsum("thd,khd->htk", query, key_block, preferred_element_type=jnp.float32)
            * score_scale
        )
        same = (seg_query[:, None] == key_seg[None, :])[None]
        scores = jnp.where(same, scores, masked_score)
        new_max = jnp.maximum(run_max, jnp.max(scores, axis=2))
        decay = jnp.exp(run_max - new_max)
        weights = jnp.where(same, jnp.exp(scores - new_max[:, :, None]), 0.0)
        run_sum = run_sum * decay + jnp.sum(weights, axis=2)
        run_acc = run_acc * decay[:, :, None] + jnp.einsum(
            "htk,khd->htd",
            weights.astype(jnp.bfloat16),
            value_block,
            preferred_element_type=jnp.float32,
        )
        return ((new_max, run_sum, run_acc), None)

    start_state = (
        jnp.full((local_heads, rows), masked_score, jnp.float32),
        jnp.zeros((local_heads, rows), jnp.float32),
        jnp.zeros((local_heads, rows, HEAD_DIM), jnp.float32),
    )
    carry = start_state
    key_piece = lax.all_gather(keys, "seq", axis=0, tiled=True)
    value_piece = lax.all_gather(values, "seq", axis=0, tiled=True)
    count = key_piece.shape[0]
    size = math.gcd(count, 1024)
    key_seg = segment_of(jnp.arange(count), lengths)
    blocks = (
        key_piece.reshape(count // size, size, local_heads, HEAD_DIM),
        value_piece.reshape(count // size, size, local_heads, HEAD_DIM),
        key_seg.reshape(count // size, size),
    )
    carry, unused = lax.scan(attend, carry, blocks)
    run_max, run_sum, run_acc = carry
    attended = (run_acc / run_sum[:, :, None]).astype(jnp.bfloat16)
    attended = attended.transpose(1, 0, 2).reshape(rows, local_heads * HEAD_DIM)
    partial_terms = jnp.dot(attended, out_weight, preferred_element_type=jnp.float32)
    summed = lax.psum_scatter(
        partial_terms.astype(jnp.bfloat16), "head", scatter_dimension=1, tiled=True
    ).astype(jnp.float32)
    mixed = (packed.astype(jnp.float32) + gate * summed).astype(jnp.bfloat16)
    outgoing = mixed[jnp.clip(got_slot, 0, rows - 1)]
    returned = lax.all_to_all(outgoing, ("pool", "seq"), split_axis=0, concat_axis=0, tiled=True)
    return returned[place]


def solution(mesh):
    in_specs = (
        P(("pool", "seq"), "head"),
        P(("pool", "seq")),
        P("pool", None),
        P("pool", None, None),
        P(None, None, "head"),
        P(),
        P("head", None),
    )
    out_specs = P(("pool", "seq"), "head")
    return jax.shard_map(local, mesh=mesh, in_specs=in_specs, out_specs=out_specs, check_vma=False)
```

profile of v0, /device:TPU:1, one launch (start us, length us, event | category | flops | bytes accessed | tf_op | source)
XLA Modules:
  0.0 247.1 jit_solution(3330954365705260041)
XLA Ops:
  6.5 0.8 and_select_fusion
  7.4 0.1 fusion.35
  7.4 0.2 reduce_window_sum.19
  7.6 0.2 select_reduce_fusion
  7.8 1.0 scatter_custom_fusion
  8.8 0.8 all_to_all.24
  9.6 18.4 %all-to-all-start = ((s32[128,2,1]{1,2,0:T(1,128)}), s32[128,2,1]{1,2,0:T(1,128)S(1)}, u32[]{:S(2)}, u32[]{:S(2)}) async-start(s32[128,2,1]{1,2,0:T(1,128)} %bitcast), calls=%async_computation | async-start | bytes 131072 | tf_op jit(solution)/shard_map/all_to_all | solution.py:40
  28.0 0.8 reduce-window.8
  28.8 0.8 slice_bitcast_fusion
  29.6 0.1 convert_reduce_fusion.2
  29.7 1.5 scatter_custom_fusion.1
  31.2 0.8 all_to_all.27
  32.0 7.4 %all-to-all-done = s32[128,2,1]{1,2,0:T(1,128)S(1)} async-done(((s32[128,2,1]{1,2,0:T(1,128)}), s32[128,2,1]{1,2,0:T(1,128)S(1)}, u32[]{:S(2)}, u32[]{:S(2)}) %all-to-all-start) | async-done | bytes 1056 | tf_op jit(solution)/shard_map/all_to_all | solution.py:40
  39.4 6.3 %all-to-all-start.1 = ((bf16[128,2,512]{2,1,0:T(2,128)(2,1)}), bf16[128,2,512]{2,1,0:T(2,128)(2,1)S(1)}, u32[]{:S(2)}, u32[]{:S(2)}) async-start(bf16[128,2,512]{2,1,0:T(2,128)(2,1)} %all_to_all.27), calls=%async_computation.1 | async-start | bytes 524288 | tf_op jit(solution)/shard_map/all_to_all | solution.py:39
  45.8 0.0 all-gather.3.cloned.1.call-start
  45.8 4.0 %fusion.31 = f32[128,6144]{1,0:T(8,128)} fusion(f32[1,8,6144]{2,1,0:T(8,128)} %param.12, s32[128]{0:T(128)S(1)} %convert_reduce_fusion.2), kind=kOutput, calls=%fused_computation.50 | convolution fusion | flops 75498496 | bytes 3342848 | tf_op jit(solution)/shard_map/dot_general | solution.py:52
  49.8 0.5 broadcast.233
  50.3 0.8 reduce.3
  51.2 0.1 all_to_all.26
  51.3 8.7 %all-to-all-done.1 = bf16[128,2,512]{2,1,0:T(2,128)(2,1)S(1)} async-done(((bf16[128,2,512]{2,1,0:T(2,128)(2,1)}), bf16[128,2,512]{2,1,0:T(2,128)(2,1)S(1)}, u32[]{:S(2)}, u32[]{:S(2)}) %all-to-all-start.1) | async-done | bytes 262176 | tf_op jit(solution)/shard_map/all_to_all | solution.py:39
  60.0 0.8 reshape.199
  60.8 1.9 scatter_custom_fusion.2
  62.7 10.7 %all_gather.9 = bf16[128,2048]{1,0:T(8,128)(2,1)S(1)} all-gather(bf16[128,512]{1,0:T(8,128)(2,1)S(1)} %scatter_custom_fusion.2), channel_id=1, replica_groups=mesh['pool'=8,'seq'=16,'head'=4] {'head'}, dimensions={1}, use_global_device_ids=true | all-gather | bytes 655360 | tf_op jit(solution)/shard_map/all_gather | solution.py:44
  73.5 0.2 convert_reduce_fusion
  73.6 0.3 fusion.21
  74.0 2.3 fusion.26
  76.2 0.7 fusion.42
  76.9 1.6 copy.26
  78.6 0.9 multiply_reduce_fusion.1
  79.5 1.6 multiply_convert_fusion.1
  81.1 0.0 all-gather.3.cloned.1.call-update
  81.2 0.0 all-gather.5.cloned.1.call-start
  81.2 0.6 slice.51
  81.8 1.6 copy.28
  83.4 0.0 all-gather.5.cloned.1.call-update
  83.4 0.2 reduce-scatter.2.cloned.1.call-start
  83.7 0.7 convert_reduce_fusion.1
  84.4 1.0 copy.27
  85.4 0.1 multiply_convert_fusion
  85.5 32.8 %all-gather.3.cloned.1.call-done = bf16[2048,4,64]{0,2,1:T(8,128)(2,1)} async-done(((bf16[128,4,64]{0,2,1:T(8,128)(2,1)}), bf16[2048,4,64]{0,2,1:T(8,128)(2,1)}) %all-gather.3.cloned.1.call-update) | async-done | bytes 1048592 | tf_op jit(solution)/shard_map/all_gather | solution.py:95
  118.3 2.3 copy.37
  120.7 39.4 %all-gather.5.cloned.1.call-done = bf16[2048,4,64]{0,2,1:T(8,128)(2,1)} async-done(((bf16[128,4,64]{0,2,1:T(8,128)(2,1)}), bf16[2048,4,64]{0,2,1:T(8,128)(2,1)}) %all-gather.5.cloned.1.call-update) | async-done | bytes 1048592 | tf_op jit(solution)/shard_map/all_gather | solution.py:96
  160.1 2.3 copy.36
  162.4 14.6 %while.15 = (s32[]{:T(128)}, f32[4,128]{1,0:T(4,128)S(1)}, f32[4,128]{1,0:T(4,128)S(1)}, f32[4,128,64]{1,2,0:T(8,128)S(1)}, s32[128]{0:T(128)S(1)}, /*index=5*/s...) while((s32[]{:T(128)}, f32[4,128]{1,0:T(4,128)S(1)}, ...), condition=%wide.region_15.16_spmd.clone, body=%wide.region_12.15_spmd.clone.sunk | while | flops 141265408 | bytes 16627353 | solution.py:105
  162.4 0.2 broadcast_compare_fusion.2
  162.6 3.0 %fusion.56 = (f32[4,128]{1,0:T(4,128)S(1)}, f32[4,1024,128]{2,1,0:T(8,128)}) fusion(pred[128,1024]{0,1:T(8,128)(4,1)S(1)} %broadcast_compare_fusion.2, bf16[128,4,64]{0,2,1:T(8,128)(2,1)S(1)} %get-tuple-element.234, bf16[2,1024,4,64]{1,3,2,0:T(8,128)(2,1)} %get-tuple-element.233, s32[]{:T(128)} %get-tuple-element.216), kind=kOutput, calls=%fused_computation.7.clone.1 | convolution fusion | flops 68681216 | bytes 2820608 | tf_op jit(solution)/shard_map/while/body/eval_jaxpr/thd,khd->htk/dot_general | solution.py:72
  165.6 2.3 fusion.57
  167.9 1.7 convolution_add_fusion.2
  169.7 0.2 broadcast_compare_fusion.2
  169.9 3.0 %fusion.56 = (f32[4,128]{1,0:T(4,128)S(1)}, f32[4,1024,128]{2,1,0:T(8,128)}) fusion(pred[128,1024]{0,1:T(8,128)(4,1)S(1)} %broadcast_compare_fusion.2, bf16[128,4,64]{0,2,1:T(8,128)(2,1)S(1)} %get-tuple-element.234, bf16[2,1024,4,64]{1,3,2,0:T(8,128)(2,1)} %get-tuple-element.233, s32[]{:T(128)} %get-tuple-element.216), kind=kOutput, calls=%fused_computation.7.clone.1 | convolution fusion | flops 68681216 | bytes 2820608 | tf_op jit(solution)/shard_map/while/body/eval_jaxpr/thd,khd->htk/dot_general | solution.py:72
  172.9 2.3 fusion.57
  175.2 0.0 copy-done.1
  175.2 1.7 convolution_add_fusion.2
  177.0 2.4 convolution_convert_fusion
  179.4 0.0 reduce-scatter.2.cloned.1.call-update
  179.4 23.5 %reduce-scatter.2.cloned.1.call-done = bf16[128,512]{1,0:T(8,128)(2,1)} async-done(((bf16[128,2048]{1,0:T(8,128)(2,1)}), bf16[128,512]{1,0:T(8,128)(2,1)}) %reduce-scatter.2.cloned.1.call-update) | async-done | bytes 131088 | tf_op jit(solution)/shard_map/reduce_scatter | solution.py:110
  202.9 0.0 copy-done.3
  202.9 1.1 add_convert_fusion
  204.0 1.9 gather_fusion
  205.8 1.7 all_to_all.30
  207.6 16.4 %all-to-all-start.2 = ((bf16[128,2,512]{2,1,0:T(2,128)(2,1)}), bf16[128,2,512]{2,1,0:T(2,128)(2,1)}, u32[]{:S(2)}, u32[]{:S(2)}) async-start(bf16[128,2,512]{2,1,0:T(2,128)(2,1)} %all_to_all.30), calls=%async_computation.3 | async-start | bytes 524288 | tf_op jit(solution)/shard_map/all_to_all | solution.py:115
  224.0 14.0 %all-to-all-done.2 = bf16[128,2,512]{2,1,0:T(2,128)(2,1)} async-done(((bf16[128,2,512]{2,1,0:T(2,128)(2,1)}), bf16[128,2,512]{2,1,0:T(2,128)(2,1)}, u32[]{:S(2)}, u32[]{:S(2)}) %all-to-all-start.2) | async-done | bytes 262176 | tf_op jit(solution)/shard_map/all_to_all | solution.py:115
  238.0 1.1 all_to_all.32
  239.1 1.5 gather_fusion.1
  (37 shorter events, 0.2 us)
Async XLA Ops:
  6.5 67.4 %copy-start = (bf16[2048,3,256]{2,0,1:T(8,128)(2,1)S(1)}, bf16[2048,3,256]{2,0,1:T(8,128)(2,1)}, u32[]{:S(2)}) copy-start(bf16[2048,3,256]{2,0,1:T(8,128)(2,1)} %param.13) | copy-start | bytes 9437188
  7.8 42.0 %copy-start.4 = (s32[128]{0:T(128)}, s32[128]{0:T(128)S(1)}, u32[]{:S(2)}) copy-start(s32[128]{0:T(128)S(1)} %compare_select_fusion.3) | copy-start | bytes 1540
  9.6 29.9 %all-to-all-start = ((s32[128,2,1]{1,2,0:T(1,128)}), s32[128,2,1]{1,2,0:T(1,128)S(1)}, u32[]{:S(2)}, u32[]{:S(2)}) async-start(s32[128,2,1]{1,2,0:T(1,128)} %bitcast), calls=%async_computation | async-start | bytes 131072 | tf_op jit(solution)/shard_map/all_to_all | solution.py:40
  28.8 21.0 %copy-start.6 = (s32[8,1]{0,1:T(1,128)}, s32[8,1]{0,1:T(1,128)S(1)}, u32[]{:S(2)}) copy-start(s32[8,1]{0,1:T(1,128)S(1)} %reduce-window.8) | copy-start | bytes 100
  39.4 20.5 %all-to-all-start.1 = ((bf16[128,2,512]{2,1,0:T(2,128)(2,1)}), bf16[128,2,512]{2,1,0:T(2,128)(2,1)S(1)}, u32[]{:S(2)}, u32[]{:S(2)}) async-start(bf16[128,2,512]{2,1,0:T(2,128)(2,1)} %all_to_all.27), calls=%async_computation.1 | async-start | bytes 524288 | tf_op jit(solution)/shard_map/all_to_all | solution.py:39
  45.8 72.6 %all-gather.3.cloned.1.call-start = ((), (), s32[]{:S(2)}) async-start(), calls=%async_computation.4 | async-start | bytes 1114112 | tf_op jit(solution)/shard_map/all_gather | solution.py:95
  62.7 11.2 %copy-start.2 = (bf16[128,512]{1,0:T(8,128)(2,1)}, bf16[128,512]{1,0:T(8,128)(2,1)S(1)}, u32[]{:S(2)}) copy-start(bf16[128,512]{1,0:T(8,128)(2,1)S(1)} %scatter_custom_fusion.2) | copy-start | bytes 393220
  81.2 78.9 %all-gather.5.cloned.1.call-start = ((), (), s32[]{:S(2)}) async-start(), calls=%async_computation.5 | async-start | bytes 1114112 | tf_op jit(solution)/shard_map/all_gather | solution.py:96
  83.4 119.5 %reduce-scatter.2.cloned.1.call-start = ((), (), s32[]{:S(2)}) async-start(), calls=%async_computation.6 | async-start | bytes 655360 | tf_op jit(solution)/shard_map/reduce_scatter | solution.py:110
  165.6 2.3 copy-start.1
  172.9 2.3 copy-start.1
  177.0 26.0 %copy-start.3 = (bf16[128,512]{1,0:T(8,128)(2,1)S(1)}, bf16[128,512]{1,0:T(8,128)(2,1)}, u32[]{:S(2)}) copy-start(bf16[128,512]{1,0:T(8,128)(2,1)} %copy-done.2) | copy-start | bytes 393220
  179.4 44.6 %copy-start.5 = (s32[128]{0:T(128)S(1)}, s32[128]{0:T(128)}, u32[]{:S(2)}) copy-start(s32[128]{0:T(128)} %copy-done.4) | copy-start | bytes 1540
  207.6 30.5 %all-to-all-start.2 = ((bf16[128,2,512]{2,1,0:T(2,128)(2,1)}), bf16[128,2,512]{2,1,0:T(2,128)(2,1)}, u32[]{:S(2)}, u32[]{:S(2)}) async-start(bf16[128,2,512]{2,1,0:T(2,128)(2,1)} %all_to_all.30), calls=%async_computation.3 | async-start | bytes 524288 | tf_op jit(solution)/shard_map/all_to_all | solution.py:115
Sparse Core Ops, SparseCore 0:
  81.3 36.9 all-gather.2
  120.4 39.6 all-gather.4
  179.5 23.3 reduce-scatter.1
where the time goes:
time: 248 us; the launch traced here: 247 us
  waiting for transfers between devices  126 us (51%)
  starting transfers between devices  41.4 us (17%)
  local copies, waits for them, and re-layouts  24.6 us (10%)
  matrix products  18.1 us (7%)
  between operations  13.4 us (5%)
  other arithmetic  12.9 us (5%)
  blocking collectives  10.7 us (4%)
    all_gather x1, waiting for transfers between devices, local(): value_piece = lax.all_gather(values, 'seq', axis=0, tiled=True)  39.4 us
    all_gather x1, waiting for transfers between devices, local(): key_piece = lax.all_gather(keys, 'seq', axis=0, tiled=True)  32.8 us
    reduce_scatter x1, waiting for transfers between devices, local(): lax.psum_scatter(partial_terms.astype(jnp.bfloat16), 'head', scatter_dime...  23.5 us
    all_to_all x1, starting transfers between devices, local(): lax.all_to_all(send_slot, ('pool', 'seq'), split_axis=0, concat_axis=0, t...  18.4 us
    all_to_all x1, starting transfers between devices, local(): lax.all_to_all(outgoing, ('pool', 'seq'), split_axis=0, concat_axis=0, ti...  16.4 us
    all_to_all x1, waiting for transfers between devices, local(): lax.all_to_all(outgoing, ('pool', 'seq'), split_axis=0, concat_axis=0, ti...  14 us
    all_gather x1, blocking collectives, local(): whole = lax.all_gather(packed, 'head', axis=1, tiled=True)  10.7 us
    all_to_all x1, waiting for transfers between devices, local(): lax.all_to_all(send_rows, ('pool', 'seq'), split_axis=0, concat_axis=0, t...  8.67 us
  transfers between devices with their start and end apart: 6, of which 6 were waited for; matrix products, arithmetic and copies ran while one was open for 6% of the time, Pallas kernels for 0%

commit v1 on v0

v1 whole, which is shorter than its diff:
```python
import functools

import jax
import jax.numpy as jnp
from jax import lax
from jax.experimental import pallas as pl
from jax.experimental.pallas import tpu as pltpu
from jax.sharding import PartitionSpec as P

MESH = pl.DeviceIdType.MESH
HEAD_DIM = 64
EPS = 1e-06
MASKED = -1e30
BF = jnp.bfloat16
F32 = jnp.float32
I32 = jnp.int32


def mm(a, b):
    return lax.dot_general(a, b, (((1,), (0,)), ((), ())), preferred_element_type=F32)


def nt(a, b):
    return lax.dot_general(a, b, (((1,), (1,)), ((), ())), preferred_element_type=F32)


def iota(shape, dim):
    return lax.broadcasted_iota(I32, shape, dim)


def onehot(cond):
    return jnp.where(cond, 1.0, 0.0).astype(BF)


def split3(x):
    hi = x.astype(BF).astype(F32)
    mid = (x - hi).astype(BF).astype(F32)
    return hi, mid, x - hi - mid


def signal(sem, **ids):
    pl.semaphore_signal(sem, inc=1, device_id=ids, device_id_type=MESH)


def remote(src, dst, send, recv, **ids):
    return pltpu.make_async_remote_copy(
        src_ref=src, dst_ref=dst, send_sem=send, recv_sem=recv, device_id=ids, device_id_type=MESH
    )


def drain(ref, sem):
    pltpu.make_async_copy(ref, ref, sem).wait()


def kernel(
    np_, ns, nh,
    lat_ref, route_ref, len_ref, gain_ref, mod_hbm, w_hbm, wo_hbm,
    out_ref,
    sb, rb, sb2, rb2, rtab, xbuf, og, modv, wv, wov, wo_all, gsrc, gbuf,
    kbuf, vbuf, scale_ref, shift_ref, acc_ref,
    stage_sem, load_sem,
    rz_s, rz_r, ry_s, ry_r, d_s, d_r, wo_s, wo_r, wc_s, wc_r, x_s, x_r, g_s, g_r,
    k_s, k_r, c_s, c_r, b_s, b_r, o_s, o_r,
):
    p, s, h = lax.axis_index("pool"), lax.axis_index("seq"), lax.axis_index("head")
    z, core = s // 2, lax.rem(s, 2)
    sib = s + 1 - 2 * core
    nz = ns // 2
    peers = np_ * ns
    me = p * ns + s
    rows, cols = lat_ref.shape
    width = cols * nh

    barrier = pltpu.get_barrier_semaphore()
    for k in range(1, ns):
        signal(barrier, seq=lax.rem(s + k, ns))
    for k in range(1, np_):
        signal(barrier, pool=lax.rem(p + k, np_))
    for k in range(1, nh):
        signal(barrier, head=lax.rem(h + k, nh))

    loads = [
        pltpu.make_async_copy(mod_hbm, modv, load_sem.at[0]),
        pltpu.make_async_copy(w_hbm, wv, load_sem.at[1]),
        pltpu.make_async_copy(wo_hbm, wov, load_sem.at[2]),
    ]
    for c in loads:
        c.start()

    rt = route_ref[...]
    r_row = jnp.broadcast_to(rt, (rows, rows))
    r_col = jnp.transpose(r_row.astype(F32)).astype(I32)
    t_row, t_col = r_row >> 7, r_col >> 7
    i0, i1 = iota((rows, rows), 0), iota((rows, rows), 1)
    same_t = t_row == t_col
    rank_row = jnp.sum(jnp.where(same_t & (i0 < i1), 1.0, 0.0), axis=0, keepdims=True).astype(I32)
    rank_col = jnp.sum(jnp.where(same_t & (i1 < i0), 1.0, 0.0), axis=1, keepdims=True).astype(I32)
    lat = lat_ref[...]
    blocks = cols // 128
    code = (rt >> 7) * (2 * blocks) + rank_row * blocks
    big = iota((peers * 2 * blocks, rows), 0)
    spread = jnp.concatenate([onehot(big == code + cb) for cb in range(blocks)], axis=1)
    stacked = jnp.concatenate([lat[:, cb * 128 : (cb + 1) * 128] for cb in range(blocks)], axis=0)
    sb[...] = mm(spread, stacked).reshape(peers, 2 * blocks, 128).astype(BF)
    rtab[me, 0] = rt[0]

    pl.semaphore_wait(barrier, ns + np_ + nh - 3)
    for k in range(1, np_):
        signal(stage_sem, pool=lax.rem(p + k, np_))
    pl.semaphore_wait(stage_sem, np_ - 1)

    for k in range(1, ns):
        remote(rtab.at[me], rtab.at[me], rz_s, rz_r, seq=lax.rem(s + k, ns)).start()

    def send_rows(k, carry):
        t = lax.rem(me + k, peers)
        remote(sb.at[t], rb.at[me], d_s, d_r, pool=t // ns, seq=lax.rem(t, ns)).start()
        return carry

    lax.fori_loop(1, peers, send_rows, 0)
    rb[me] = sb[me]

    loads[2].wait()
    half = wov.shape[0] // 2
    mine = pl.ds(pl.multiple_of(core * half, half), half)
    other = pl.ds(pl.multiple_of((1 - core) * half, half), half)
    wo_sends = []
    for k in range(1, nh):
        t = lax.rem(h + k, nh)
        cp = remote(
            wov.at[mine, pl.ds(pl.multiple_of(t * cols, cols), cols)], wo_all.at[h, mine],
            wo_s.at[k], wo_r.at[k], head=t,
        )
        cp.start()
        wo_sends.append(cp)
    wo_all[h] = wov[:, pl.ds(pl.multiple_of(h * cols, cols), cols)]

    drain(rtab.at[pl.ds(0, ns - 1)], rz_r)
    own_line = rtab.at[pl.ds(pl.multiple_of(p * ns, ns), ns)]
    for k in range(1, np_):
        remote(own_line, own_line, ry_s, ry_r, pool=lax.rem(p + k, np_)).start()

    ends = []
    total = 0
    for k in range(8):
        total = total + len_ref[0, k]
        ends.append(total)
    starts = [0] + ends[:7]

    def lane_row(n, values, offset, period):
        lane = iota((1, n), 1)
        out = jnp.zeros((1, n), I32)
        for k in range(8):
            hit = (lane & (period - 1)) == offset + k
            out = jnp.where(hit, values[k], out)
        return out

    pos32 = s * rows + iota((rows, 32), 0)
    pick = onehot(
        (pos32 >= lane_row(32, starts, 0, 8)) & (pos32 < lane_row(32, ends, 0, 8)) & (iota((rows, 32), 1) < 24)
    )
    loads[0].wait()
    step = 1024
    for c in range(0, 2 * width, step):
        hi, mid, lo = split3(modv[:, c : c + step])
        table = jnp.concatenate([hi, mid, lo, jnp.zeros_like(lo)], axis=0).astype(BF)
        part = mm(pick, table)
        if c < width:
            shift_ref[:, c : c + step] = part
        else:
            scale_ref[:, c - width : c - width + step] = 1.0 + part
    gsrc[:, :cols] = modv[:, pl.ds(pl.multiple_of(2 * width + h * cols, cols), cols)]
    lane = iota((1, 128), 1)
    end_l, start_l = jnp.zeros((1, 128), I32), jnp.zeros((1, 128), I32)
    for k in range(8):
        hit = lane == p * 8 + k
        end_l = jnp.where(hit, ends[k], end_l)
        start_l = jnp.where(hit, starts[k], start_l)
    gsrc[:, cols : cols + 128] = jnp.broadcast_to(end_l.astype(F32), (8, 128))
    gsrc[:, cols + 128 :] = jnp.broadcast_to(start_l.astype(F32), (8, 128))
    gbuf[p] = gsrc[...]

    drain(rtab.at[pl.ds(0, (np_ - 1) * ns)], ry_r)
    table = rtab[...].reshape(peers, rows)
    here = (table >> 7) == me
    before = mm(onehot(here), onehot(i0 < i1))
    slot1 = (table & 127).astype(F32) + 1.0
    place_u, spread_b = [], None
    wide = iota((peers, peers * 2 * blocks), 1)
    wide0 = iota((peers, peers * 2 * blocks), 0)
    shift_bits = {1: 1, 2: 2, 4: 3}[blocks]
    for k in range(2):
        zk = jnp.where(here & (before == float(k)), slot1, 0.0)
        col_k = jnp.sum(zk, axis=1, keepdims=True).astype(I32) - 1
        row_k = nt(jnp.ones((8, rows), BF), zk.astype(BF))[0:1].astype(I32) - 1
        place_u.append(onehot(col_k == iota((peers, rows), 1)))
        ut = onehot(iota((rows, peers), 0) == row_k)
        ek = onehot(((wide >> shift_bits) == wide0) & (((wide >> (shift_bits - 1)) & 1) == k))
        part = mm(ut, ek)
        spread_b = part if spread_b is None else spread_b + part
    narrow = iota((rows, peers * 2 * blocks), 1) & (blocks - 1)
    takes = [jnp.where(narrow == cb, spread_b, 0.0).astype(BF) for cb in range(blocks)]

    drain(rb.at[pl.ds(0, peers - 1)], d_r)
    arrived = rb[...].astype(F32).reshape(peers * 2 * blocks, 128).astype(BF)
    for cb in range(blocks):
        xbuf[h, :, cb * 128 : (cb + 1) * 128] = mm(takes[cb], arrived).astype(BF)

    right, left = lax.rem(h + 1, nh), lax.rem(h + nh - 1, nh)
    hr = rows // 2

    def xpart(b, half_):
        return xbuf.at[b, pl.ds(half_ * hr, hr)]

    xs = []
    for half_ in (0, 1):
        a = remote(xpart(h, half_), xpart(h, half_), x_s.at[half_], x_r.at[half_], head=right)
        a.start()
        b = remote(xpart(h, 1 - half_), xpart(h, 1 - half_), x_s.at[2 + half_], x_r.at[2 + half_], head=left)
        b.start()
        xs += [a, b]
    xs[0].wait_recv()
    a = remote(xpart(left, 0), xpart(left, 0), x_s.at[4], x_r.at[4], head=right)
    a.start()
    xs[1].wait_recv()
    b = remote(xpart(right, 1), xpart(right, 1), x_s.at[5], x_r.at[5], head=left)
    b.start()

    for k in range(1, np_):
        remote(gsrc, gbuf.at[p], g_s, g_r, pool=lax.rem(p + k, np_)).start()
    wo_fwd = []
    for k in range(1, nh):
        wo_sends[k - 1].wait_recv()
        src_h = lax.rem(h + nh - k, nh)
        cp = remote(wo_all.at[src_h, mine], wo_all.at[src_h, mine], wc_s.at[k], wc_r.at[k], seq=sib)
        cp.start()
        wo_fwd.append(cp)

    for c in (xs[2], xs[3], a, b):
        c.wait_recv()
    for c in xs + [a, b]:
        c.wait_send()

    feats = jnp.concatenate([xbuf[i] for i in range(nh)], axis=1).astype(F32)
    centred = feats - jnp.mean(feats, axis=1, keepdims=True)
    var = jnp.mean(centred * centred, axis=1, keepdims=True)
    normed = (centred * lax.rsqrt(var + EPS) * scale_ref[...] + shift_ref[...]).astype(BF)
    loads[1].wait()
    hw = wv.shape[2]
    heads = hw // HEAD_DIM
    head_same = onehot((iota((hw, hw), 0) >> 6) == (iota((hw, hw), 1) >> 6))

    def rms(v, gain):
        sq = v * v
        hi = sq.astype(BF)
        lo = (sq - hi.astype(F32)).astype(BF)
        mean_sq = (mm(hi, head_same) + mm(lo, head_same)) * (1.0 / HEAD_DIM)
        return (v * lax.rsqrt(mean_sq + EPS) * gain).astype(BF)

    gains = jnp.concatenate([gain_ref[...]] * heads, axis=1)
    kbuf[s] = rms(mm(normed, wv[1]), gains[1:2])
    vbuf[s] = jnp.transpose(mm(normed, wv[2])).astype(BF)

    def zat(d):
        return lax.rem(z + d + nz, nz)

    bufs = (kbuf, vbuf)
    live, sends, sibs = {}, [], {}

    def pass_on(src_z, j, d, hop):
        block = bufs[j].at[src_z * 2 + core]
        cp = remote(
            block, block, k_s.at[d, hop, j], k_r.at[d, hop, j], seq=zat(1 if d == 0 else -1) * 2 + core
        )
        cp.start()
        live[d, hop, j] = cp
        sends.append(cp)

    def to_sib(src_z, j, d, hop):
        block = bufs[j].at[src_z * 2 + core]
        cp = remote(block, block, c_s.at[d, hop, j], c_r.at[d, hop, j], seq=sib)
        cp.start()
        sibs[d, hop, j] = cp

    for j in (0, 1):
        pass_on(z, j, 0, 1)
        pass_on(z, j, 1, 1)
    for j in (0, 1):
        to_sib(z, j, 0, 0)

    query = rms(mm(normed, wv[0]), gains[0:1])
    q_t = jnp.transpose(query.astype(F32) * 0.125)
    feat_head = iota((hw, rows), 0) >> 6
    q_bd = jnp.concatenate([jnp.where(feat_head == i, q_t, 0.0) for i in range(heads)], axis=1).astype(BF)
    q_pos = s * rows + (iota((1, heads * rows), 1) & (rows - 1))
    q_start, q_end = jnp.zeros_like(q_pos), jnp.zeros_like(q_pos)
    for k in range(8):
        inside = (q_pos >= starts[k]) & (q_pos < ends[k])
        q_start = jnp.where(inside, starts[k], q_start)
        q_end = jnp.where(inside, ends[k], q_end)

    def attend(src_z, state):
        keys = kbuf[pl.ds(src_z * 2, 2)].reshape(2 * rows, hw)
        vals = jnp.concatenate([vbuf[src_z * 2], vbuf[src_z * 2 + 1]], axis=1)
        scores = mm(keys, q_bd)
        key_pos = src_z * (2 * rows) + iota(scores.shape, 0)
        scores = jnp.where((key_pos >= q_start) & (key_pos < q_end), scores, MASKED)
        top = jnp.max(scores, axis=0, keepdims=True)
        if state is not None:
            top = jnp.maximum(top, state[0])
        weights = jnp.exp(scores - top)
        summed = jnp.sum(weights, axis=0, keepdims=True)
        mixed = mm(vals, weights.astype(BF))
        if state is not None:
            decay = jnp.exp(state[0] - top)
            summed = summed + state[1] * decay
        for i in range(heads):
            f, q = slice(i * HEAD_DIM, (i + 1) * HEAD_DIM), slice(i * rows, (i + 1) * rows)
            if state is None:
                acc_ref[f, :] = mixed[f, q]
            else:
                acc_ref[f, :] = acc_ref[f, :] * decay[:, q] + mixed[f, q]
        return top, summed

    last = nz // 2
    ready = [(z, [(0, 0, 0), (0, 0, 1)])]
    state = None
    for hop in range(1, last + 1):
        coming = {}
        for j in (0, 1):
            for d in (0, 1):
                if (d, hop, j) not in live:
                    continue
                src_z = zat(-hop if d == 0 else hop)
                live[d, hop, j].wait_recv()
                if hop + 1 < last or (hop + 1 == last and d == j):
                    pass_on(src_z, j, d, hop + 1)
                to_sib(src_z, j, d, hop)
                coming.setdefault(d if hop < last else 0, (src_z, []))[1].append((d, hop, j))
        for src_z, keys_ in ready:
            for key in keys_:
                sibs[key].wait_recv()
            state = attend(src_z, state)
        ready = list(coming.values())
    for src_z, keys_ in ready:
        for key in keys_:
            sibs[key].wait_recv()
        state = attend(src_z, state)

    total_w = state[1]
    att = []
    for i in range(heads):
        f, q = slice(i * HEAD_DIM, (i + 1) * HEAD_DIM), slice(i * rows, (i + 1) * rows)
        att.append((acc_ref[f, :] / total_w[:, q]).astype(BF).astype(F32))
    att = jnp.concatenate(att, axis=0)
    ob = hw // 128
    att_st = jnp.concatenate(
        [jnp.transpose(att[cb * 128 : (cb + 1) * 128]) for cb in range(ob)], axis=0
    ).astype(BF)

    n2 = peers * 2 * ob
    ob_bits = {1: 0, 2: 1}[ob]
    tall, tall1 = iota((n2, peers), 0), iota((n2, peers), 1)
    picked = None
    for k in range(2):
        e2 = onehot(((tall >> (ob_bits + 1)) == tall1) & (((tall >> ob_bits) & 1) == k))
        part = mm(e2, place_u[k])
        picked = part if picked is None else picked + part
    lowbit = iota((n2, rows), 0) & (ob - 1)
    a3 = jnp.concatenate([jnp.where(lowbit == cb, picked, 0.0) for cb in range(ob)], axis=1).astype(BF)
    sb2[...] = mm(a3, att_st).reshape(peers, 2 * ob, 128).astype(BF)

    def send_back(k, carry):
        t = lax.rem(me + k, peers)
        remote(sb2.at[t], rb2.at[me], b_s, b_r, pool=t // ns, seq=lax.rem(t, ns)).start()
        return carry

    lax.fori_loop(1, peers, send_back, 0)
    rb2[me] = sb2[me]

    drain(gbuf.at[pl.ds(0, np_ - 1)], g_r)
    info = gbuf[...].reshape(np_ * 8, cols + 256)
    end_row = jnp.sum(gbuf[:, 0, cols : cols + 128], axis=0, keepdims=True)[:, : np_ * 8]
    start_row = jnp.sum(gbuf[:, 0, cols + 128 :], axis=0, keepdims=True)[:, : np_ * 8]
    group_bits = {2048: 11, 1024: 10, 512: 9}[ns * rows]
    base = r_col[:, : np_ * 8]
    pos = (base & (ns * rows - 1)).astype(F32)
    own = (base >> group_bits) == (iota((rows, np_ * 8), 1) >> 3)
    pick_g = onehot(own & (pos >= start_row) & (pos < end_row))
    gate = None
    for piece in split3(info[:, :cols]):
        part = mm(pick_g, piece.astype(BF))
        gate = part if gate is None else gate + part

    code2 = t_col * (2 * ob) + rank_col * ob
    drain(rb2.at[pl.ds(0, peers - 1)], b_r)
    back = rb2[...].astype(F32).reshape(n2, 128).astype(BF)
    wide2 = iota((rows, n2), 1)
    code2 = jnp.concatenate([code2] * (n2 // rows), axis=1)
    for cb in range(ob):
        og[h, :, cb * 128 : (cb + 1) * 128] = mm(onehot(wide2 == code2 + cb), back).astype(BF)
    os_ = []
    for k in (2, 1, 3) if nh == 4 else range(1, nh):
        cp = remote(og.at[h], og.at[h], o_s.at[k], o_r.at[k], head=lax.rem(h + k, nh))
        cp.start()
        os_.append(cp)
    for c in wo_fwd:
        c.wait_recv()
    for c in os_:
        c.wait_recv()
    projected = None
    for i in range(nh):
        part = mm(og[i], wo_all[i])
        projected = part if projected is None else projected + part
    out_ref[...] = (lat_ref[...].astype(F32) + gate * projected).astype(BF)

    for c in os_ + wo_fwd + wo_sends + sends + list(sibs.values()):
        c.wait_send()
    drain(rtab.at[pl.ds(0, ns - 1)], rz_s)
    drain(rtab.at[pl.ds(0, (np_ - 1) * ns)], ry_s)
    drain(rb.at[pl.ds(0, peers - 1)], d_s)
    drain(rb2.at[pl.ds(0, peers - 1)], b_s)
    drain(gbuf.at[pl.ds(0, np_ - 1)], g_s)


def local(np_, ns, nh, latents, route, seg_lengths, modulation, qkv_weight, qk_gain, out_weight):
    rows, cols = latents.shape
    peers = np_ * ns
    blocks = cols // 128
    hw = qkv_weight.shape[2]
    ob = hw // 128
    width = cols * nh
    vm = pl.BlockSpec(memory_space=pltpu.VMEM)
    hbm = pl.BlockSpec(memory_space=pl.ANY)
    D = pltpu.SemaphoreType.DMA
    V = pltpu.VMEM
    return pl.pallas_call(
        functools.partial(kernel, np_, ns, nh),
        out_shape=jax.ShapeDtypeStruct((rows, cols), BF),
        in_specs=[vm, vm, pl.BlockSpec(memory_space=pltpu.SMEM), vm, hbm, hbm, hbm],
        out_specs=vm,
        scratch_shapes=[
            V((peers, 2 * blocks, 128), BF), V((peers, 2 * blocks, 128), BF),
            V((peers, 2 * ob, 128), BF), V((peers, 2 * ob, 128), BF),
            V((peers, 1, 128), I32),
            V((nh, rows, cols), BF), V((nh, rows, hw), BF),
            V((8, 3 * width), F32), V((3, width, hw), BF), V((hw, width), BF), V((nh, hw, cols), BF),
            V((8, cols + 256), F32), V((np_, 8, cols + 256), F32),
            V((ns, rows, hw), BF), V((ns, hw, rows), BF),
            V((rows, width), F32), V((rows, width), F32), V((hw, rows), F32),
            pltpu.SemaphoreType.REGULAR, D((3,)),
            D, D, D, D, D, D, D((4,)), D((4,)), D((4,)), D((4,)), D((6,)), D((6,)), D, D,
            D((2, 5, 2)), D((2, 5, 2)), D((2, 5, 2)), D((2, 5, 2)), D, D, D((4,)), D((4,)),
        ],
        compiler_params=pltpu.CompilerParams(
            collective_id=0, has_side_effects=True, vmem_limit_bytes=56 << 20
        ),
    )(
        latents, route.reshape(1, rows), seg_lengths, qk_gain, modulation[0],
        qkv_weight.transpose(1, 0, 2), out_weight,
    )


def solution(mesh):
    np_, ns, nh = mesh.shape["pool"], mesh.shape["seq"], mesh.shape["head"]
    return jax.shard_map(
        functools.partial(local, np_, ns, nh),
        mesh=mesh,
        in_specs=(
            P(("pool", "seq"), "head"), P(("pool", "seq")), P("pool", None), P("pool", None, None),
            P(None, None, "head"), P(), P("head", None),
        ),
        out_specs=P(("pool", "seq"), "head"),
        check_vma=False,
    )
```

time: 248 us -> 78.1 us (0.31)
  waiting for transfers between devices: 126 us -> 0 us
  Pallas kernels: 0 us -> 76.3 us
  starting transfers between devices: 41.4 us -> 0 us
  local copies, waits for them, and re-layouts: 24.6 us -> 1.57 us
  matrix products: 18.1 us -> 0 us
  between operations: 13.4 us -> 0.01 us
  other arithmetic: 12.9 us -> 0 us
  blocking collectives: 10.7 us -> 0 us
    pallas_call x0 -> x1, Pallas kernels: none -> 76.3 us  [local(): pl.pallas_call(functools.partial(kernel, np_, ns, nh), out_shape=jax.Shap...]
    all_gather x2 -> x0, waiting for transfers between devices: 72.2 us -> none  [the longest x1 39.4 us: local(): value_piece = lax.all_gather(values, 'seq', axis=0, tiled=True)]
    all_to_all x3 -> x0, starting transfers between devices: 41.1 us -> none  [the longest x1 18.4 us: local(): lax.all_to_all(send_slot, ('pool', 'seq'), split_axis=0, concat_axis=0, t...]
    all_to_all x3 -> x0, waiting for transfers between devices: 30.1 us -> none  [the longest x1 14 us: local(): lax.all_to_all(outgoing, ('pool', 'seq'), split_axis=0, concat_axis=0, ti...]
    reduce_scatter x1 -> x0, waiting for transfers between devices: 23.5 us -> none  [local(): lax.psum_scatter(partial_terms.astype(jnp.bfloat16), 'head', scatter_dime...]
    dot_general x7 -> x0, matrix products: 18.1 us -> none  [the longest x2 6.01 us: attend(): jnp.einsum('thd,khd->htk', query, key_block, preferred_element_type=jnp.f...]
    all_gather x1 -> x0, blocking collectives: 10.7 us -> none  [local(): whole = lax.all_gather(packed, 'head', axis=1, tiled=True)]
    reduce_sum x9 -> x0, other arithmetic: 6.88 us -> none  [the longest x2 4.53 us: attend(): run_sum = run_sum * decay + jnp.sum(weights, axis=2)]
  transfers between devices with their start and end apart: 6 -> 0, of which waited for: 6 -> 0; matrix products, arithmetic and copies ran while one was open for 6% -> 0% of each run, Pallas kernels for 0% -> 0%
where the time goes in v1:
time: 78.1 us; the launch traced here: 77.9 us
  Pallas kernels  76.3 us (98%)
  local copies, waits for them, and re-layouts  1.57 us (2%)
    pallas_call x1, Pallas kernels, local(): pl.pallas_call(functools.partial(kernel, np_, ns, nh), out_shape=jax.Shap...  76.3 us
    unnamed x1, local copies, waits for them, and re-layouts  1.57 us

profile of v1, /device:TPU:1, one launch (start us, length us, event | category | flops | bytes accessed | tf_op | source)
XLA Modules:
  0.0 77.9 jit_solution(6364197239516537916)
XLA Ops:
  0.0 76.3 %shard_map.73 = bf16[128,512]{1,0:T(8,128)(2,1)} custom-call(bf16[128,512]{1,0:T(8,128)(2,1)} %lat_ref.1, s32[1,128]{1,0:T(1,128)} %bitcast.5, s32[1,8]{1,0:T(1,128)} %len_ref.1, f32[2,64]{1,0:T(2,128)} %gain_ref.1, f32[8,6144]{1,0:T(8,128)} %bitcast.4, bf16[3,2048,256]{2,1,0:T(8,128)(2,1)} %bitcast.3, bf16[256,2048]{1,0:T(8,128)(2,1)} %wo_hbm.1), custom_call_target="tpu_custom_call" | custom-call | tf_op jit(solution)/shard_map/pallas_call | solution.py:437
  76.4 1.6 %copy.9 = bf16[128,512]{1,0:T(8,128)(2,1)} copy(bf16[128,512]{1,0:T(8,128)(2,1)} %shard_map.73) | data formatting | bytes 262144

commit v2 on v1

--- a/solution.py
+++ b/solution.py
@@ -54,13 +54,13 @@
 
 def kernel(
     np_, ns, nh,
-    lat_ref, route_ref, len_ref, gain_ref, mod_hbm, w_hbm, wo_hbm,
+    lat_hbm, route_hbm, len_hbm, gain_hbm, mod_hbm, w_hbm, wo_hbm,
     out_ref,
-    sb, rb, sb2, rb2, rtab, xbuf, og, modv, wv, wov, wo_all, gsrc, gbuf,
-    kbuf, vbuf, scale_ref, shift_ref, acc_ref,
+    lat_ref, route_ref, len_ref, gain_ref, sb, rb, sb2, rb2, rtab, xbuf, og, modv, wv, wov, wo_all, gsrc, gbuf,
+    kv_send, kv_buf, q_send, q_buf, back_ref, scale_ref, shift_ref, acc_ref,
     stage_sem, load_sem,
     rz_s, rz_r, ry_s, ry_r, d_s, d_r, wo_s, wo_r, wc_s, wc_r, x_s, x_r, g_s, g_r,
-    k_s, k_r, c_s, c_r, b_s, b_r, o_s, o_r,
+    k_s, k_r, c_s, c_r, q_s, q_r, b_s, b_r, o_s, o_r,
 ):
     p, s, h = lax.axis_index("pool"), lax.axis_index("seq"), lax.axis_index("head")
     z, core = s // 2, lax.rem(s, 2)
@@ -79,6 +79,14 @@
     for k in range(1, nh):
         signal(barrier, head=lax.rem(h + k, nh))
 
+    first = [
+        pltpu.make_async_copy(route_hbm, route_ref, load_sem.at[3]),
+        pltpu.make_async_copy(lat_hbm, lat_ref, load_sem.at[4]),
+        pltpu.make_async_copy(len_hbm, len_ref, load_sem.at[5]),
+        pltpu.make_async_copy(gain_hbm, gain_ref, load_sem.at[6]),
+    ]
+    for c in first:
+        c.start()
     loads = [
         pltpu.make_async_copy(mod_hbm, modv, load_sem.at[0]),
         pltpu.make_async_copy(w_hbm, wv, load_sem.at[1]),
@@ -87,6 +95,7 @@
     for c in loads:
         c.start()
 
+    first[0].wait()
     rt = route_ref[...]
     r_row = jnp.broadcast_to(rt, (rows, rows))
     r_col = jnp.transpose(r_row.astype(F32)).astype(I32)
@@ -95,6 +104,7 @@
     same_t = t_row == t_col
     rank_row = jnp.sum(jnp.where(same_t & (i0 < i1), 1.0, 0.0), axis=0, keepdims=True).astype(I32)
     rank_col = jnp.sum(jnp.where(same_t & (i1 < i0), 1.0, 0.0), axis=1, keepdims=True).astype(I32)
+    first[1].wait()
     lat = lat_ref[...]
     blocks = cols // 128
     code = (rt >> 7) * (2 * blocks) + rank_row * blocks
@@ -107,18 +117,29 @@
     pl.semaphore_wait(barrier, ns + np_ + nh - 3)
     for k in range(1, np_):
         signal(stage_sem, pool=lax.rem(p + k, np_))
-    pl.semaphore_wait(stage_sem, np_ - 1)
 
     for k in range(1, ns):
         remote(rtab.at[me], rtab.at[me], rz_s, rz_r, seq=lax.rem(s + k, ns)).start()
 
-    def send_rows(k, carry):
-        t = lax.rem(me + k, peers)
-        remote(sb.at[t], rb.at[me], d_s, d_r, pool=t // ns, seq=lax.rem(t, ns)).start()
+    def send_row(dp, ds):
+        tp, ts = lax.rem(p + dp, np_), lax.rem(s + ds, ns)
+        remote(sb.at[tp * ns + ts], rb.at[me], d_s, d_r, pool=tp, seq=ts).start()
+
+    for k in range(1, ns):
+        send_row(0, k)
+    for k in range(1, np_):
+        send_row(k, 0)
+    rb[me] = sb[me]
+    pl.semaphore_wait(stage_sem, np_ - 1)
+
+    def send_rows(i, carry):
+        a, b = i // (np_ - 1), lax.rem(i, np_ - 1)
+        ds = lax.rem(ns // 2 + jnp.where(lax.rem(a, 2) == 0, a // 2, ns - (a + 1) // 2), ns)
+        dp = lax.rem(np_ // 2 + jnp.where(lax.rem(b, 2) == 0, b // 2, np_ - (b + 1) // 2), np_)
+        send_row(dp, ds)
         return carry
 
-    lax.fori_loop(1, peers, send_rows, 0)
-    rb[me] = sb[me]
+    lax.fori_loop(0, (ns - 1) * (np_ - 1), send_rows, 0)
 
     loads[2].wait()
     half = wov.shape[0] // 2
@@ -140,6 +161,8 @@
     for k in range(1, np_):
         remote(own_line, own_line, ry_s, ry_r, pool=lax.rem(p + k, np_)).start()
 
+    first[2].wait()
+    first[3].wait()
     ends = []
     total = 0
     for k in range(8):
@@ -185,15 +208,13 @@
     here = (table >> 7) == me
     before = mm(onehot(here), onehot(i0 < i1))
     slot1 = (table & 127).astype(F32) + 1.0
-    place_u, spread_b = [], None
+    spread_b = None
     wide = iota((peers, peers * 2 * blocks), 1)
     wide0 = iota((peers, peers * 2 * blocks), 0)
     shift_bits = {1: 1, 2: 2, 4: 3}[blocks]
     for k in range(2):
         zk = jnp.where(here & (before == float(k)), slot1, 0.0)
-        col_k = jnp.sum(zk, axis=1, keepdims=True).astype(I32) - 1
         row_k = nt(jnp.ones((8, rows), BF), zk.astype(BF))[0:1].astype(I32) - 1
-        place_u.append(onehot(col_k == iota((peers, rows), 1)))
         ut = onehot(iota((rows, peers), 0) == row_k)
         ek = onehot(((wide >> shift_bits) == wide0) & (((wide >> (shift_bits - 1)) & 1) == k))
         part = mm(ut, ek)
@@ -207,24 +228,22 @@
         xbuf[h, :, cb * 128 : (cb + 1) * 128] = mm(takes[cb], arrived).astype(BF)
 
     right, left = lax.rem(h + 1, nh), lax.rem(h + nh - 1, nh)
-    hr = rows // 2
-
-    def xpart(b, half_):
-        return xbuf.at[b, pl.ds(half_ * hr, hr)]
-
-    xs = []
-    for half_ in (0, 1):
-        a = remote(xpart(h, half_), xpart(h, half_), x_s.at[half_], x_r.at[half_], head=right)
-        a.start()
-        b = remote(xpart(h, 1 - half_), xpart(h, 1 - half_), x_s.at[2 + half_], x_r.at[2 + half_], head=left)
-        b.start()
-        xs += [a, b]
-    xs[0].wait_recv()
-    a = remote(xpart(left, 0), xpart(left, 0), x_s.at[4], x_r.at[4], head=right)
-    a.start()
-    xs[1].wait_recv()
-    b = remote(xpart(right, 1), xpart(right, 1), x_s.at[5], x_r.at[5], head=left)
-    b.start()
+    hr = rows // 4
+
+    def xsend(b, part, i, to):
+        block = xbuf.at[b, pl.ds(part * hr, hr)]
+        cp = remote(block, block, x_s.at[i], x_r.at[i], head=to)
+        cp.start()
+        return cp
+
+    to_right = [xsend(h, part, i, right) for i, part in enumerate((0, 1, 2, 3))]
+    to_left = [xsend(h, part, 4 + i, left) for i, part in enumerate((2, 3, 0, 1))]
+    onward = []
+    for i in range(2):
+        to_right[i].wait_recv()
+        onward.append(xsend(left, i, 8 + i, right))
+        to_left[i].wait_recv()
+        onward.append(xsend(right, 2 + i, 10 + i, left))
 
     for k in range(1, np_):
         remote(gsrc, gbuf.at[p], g_s, g_r, pool=lax.rem(p + k, np_)).start()
@@ -236,9 +255,9 @@
         cp.start()
         wo_fwd.append(cp)
 
-    for c in (xs[2], xs[3], a, b):
+    for c in to_right[2:] + to_left[2:] + onward:
         c.wait_recv()
-    for c in xs + [a, b]:
+    for c in to_right + to_left + onward:
         c.wait_send()
 
     feats = jnp.concatenate([xbuf[i] for i in range(nh)], axis=1).astype(F32)
@@ -258,51 +277,89 @@
         return (v * lax.rsqrt(mean_sq + EPS) * gain).astype(BF)
 
     gains = jnp.concatenate([gain_ref[...]] * heads, axis=1)
-    kbuf[s] = rms(mm(normed, wv[1]), gains[1:2])
-    vbuf[s] = jnp.transpose(mm(normed, wv[2])).astype(BF)
+    keys = rms(mm(normed, wv[1]), gains[1:2])
+    vals = mm(normed, wv[2]).astype(BF)
+    from_lane, to_lane = iota((hw, 2 * hw), 0), iota((hw, 2 * hw), 1)
+    at_lane = (from_lane >> 6) * 128 + (from_lane & 63)
+    kv = mm(keys, onehot(to_lane == at_lane)) + mm(vals, onehot(to_lane == at_lane + 64))
+    for i in range(heads):
+        kv_send[i] = kv[:, i * 128 : (i + 1) * 128].astype(BF)
 
     def zat(d):
         return lax.rem(z + d + nz, nz)
 
-    bufs = (kbuf, vbuf)
-    live, sends, sibs = {}, [], {}
-
-    def pass_on(src_z, j, d, hop):
-        block = bufs[j].at[src_z * 2 + core]
-        cp = remote(
-            block, block, k_s.at[d, hop, j], k_r.at[d, hop, j], seq=zat(1 if d == 0 else -1) * 2 + core
-        )
-        cp.start()
-        live[d, hop, j] = cp
-        sends.append(cp)
-
-    def to_sib(src_z, j, d, hop):
-        block = bufs[j].at[src_z * 2 + core]
-        cp = remote(block, block, c_s.at[d, hop, j], c_r.at[d, hop, j], seq=sib)
-        cp.start()
-        sibs[d, hop, j] = cp
-
-    for j in (0, 1):
-        pass_on(z, j, 0, 1)
-        pass_on(z, j, 1, 1)
-    for j in (0, 1):
-        to_sib(z, j, 0, 0)
+    my_head, my_quarter = z // 2, lax.rem(z, 2) * 2 + core
+    near = []
+    for d in range(1, nz // 2 + 1):
+        near += [d, nz - d] if 2 * d < nz else [d]
+    kv_live, sibs = {}, {}
+    for d in reversed(near):
+        to = zat(d)
+        kv_live[d] = remote(kv_send.at[to // 2], kv_buf.at[s], k_s.at[d], k_r.at[d], seq=to * 2 + core)
+        kv_live[d].start()
+
+    def to_sib(d):
+        block = kv_buf.at[zat(-d) * 2 + core]
+        sibs[d] = remote(block, block, c_s.at[d], c_r.at[d], seq=sib)
+        sibs[d].start()
+
+    kv_buf[s] = kv_send[my_head]
+    to_sib(0)
 
     query = rms(mm(normed, wv[0]), gains[0:1])
-    q_t = jnp.transpose(query.astype(F32) * 0.125)
-    feat_head = iota((hw, rows), 0) >> 6
-    q_bd = jnp.concatenate([jnp.where(feat_head == i, q_t, 0.0) for i in range(heads)], axis=1).astype(BF)
-    q_pos = s * rows + (iota((1, heads * rows), 1) & (rows - 1))
+    q_send[...] = jnp.transpose(query.astype(F32) * 0.125).astype(BF).reshape(heads, HEAD_DIM, rows)
+    quarter, part_of = s // 4, lax.rem(s, 4)
+
+    def q_copy(i):
+        to = i * 4 + quarter
+        return to, remote(q_send.at[i], q_buf.at[part_of], q_s.at[i], q_r.at[part_of], seq=to)
+
+    for i in range(heads):
+        to, cp = q_copy(i)
+
+        @pl.when(to != s)
+        def _():
+            cp.start()
+
+        @pl.when(to == s)
+        def _():
+            q_buf[part_of] = q_send[i]
+
+    n2 = peers * 4
+    tall, tall1 = iota((n2, peers), 0), iota((n2, peers), 1)
+    backs = [[], []]
+    for t in range(4):
+        here_t = (table >> 7) == p * ns + my_quarter * 4 + t
+        before_t = mm(onehot(here_t), onehot(i0 < i1))
+        e_t = onehot(tall == tall1 * 4 + t)
+        for k in range(2):
+            zk = jnp.where(here_t & (before_t == float(k)), slot1, 0.0)
+            col_k = jnp.sum(zk, axis=1, keepdims=True).astype(I32) - 1
+            backs[k].append(mm(e_t, onehot(col_k == iota((peers, rows), 1))).astype(BF))
+    for k in range(2):
+        for t in range(4):
+            back_ref[k, :, t * rows : (t + 1) * rows] = backs[k][t]
+
+    q_pos = my_quarter * (4 * rows) + iota((1, 4 * rows), 1)
     q_start, q_end = jnp.zeros_like(q_pos), jnp.zeros_like(q_pos)
     for k in range(8):
         inside = (q_pos >= starts[k]) & (q_pos < ends[k])
         q_start = jnp.where(inside, starts[k], q_start)
         q_end = jnp.where(inside, ends[k], q_end)
 
+    for i in range(4):
+        @pl.when(my_quarter * 4 + i != s)
+        def _():
+            remote(q_send.at[0], q_buf.at[i], q_s.at[0], q_r.at[i], seq=sib).wait_recv()
+
+    q_pad = jnp.concatenate(
+        [jnp.concatenate([q_buf[i] for i in range(4)], axis=1), jnp.zeros((HEAD_DIM, 4 * rows), BF)], axis=0
+    )
+
     def attend(src_z, state):
-        keys = kbuf[pl.ds(src_z * 2, 2)].reshape(2 * rows, hw)
-        vals = jnp.concatenate([vbuf[src_z * 2], vbuf[src_z * 2 + 1]], axis=1)
-        scores = mm(keys, q_bd)
+        block = kv_buf[pl.ds(src_z * 2, 2)].reshape(2 * rows, 2 * HEAD_DIM)
+        values_t = jnp.transpose(block.astype(F32))[HEAD_DIM:].astype(BF)
+        scores = mm(block, q_pad)
         key_pos = src_z * (2 * rows) + iota(scores.shape, 0)
         scores = jnp.where((key_pos >= q_start) & (key_pos < q_end), scores, MASKED)
         top = jnp.max(scores, axis=0, keepdims=True)
@@ -310,65 +367,34 @@
             top = jnp.maximum(top, state[0])
         weights = jnp.exp(scores - top)
         summed = jnp.sum(weights, axis=0, keepdims=True)
-        mixed = mm(vals, weights.astype(BF))
-        if state is not None:
+        mixed = mm(values_t, weights.astype(BF))
+        if state is None:
+            acc_ref[...] = mixed
+        else:
             decay = jnp.exp(state[0] - top)
             summed = summed + state[1] * decay
-        for i in range(heads):
-            f, q = slice(i * HEAD_DIM, (i + 1) * HEAD_DIM), slice(i * rows, (i + 1) * rows)
-            if state is None:
-                acc_ref[f, :] = mixed[f, q]
-            else:
-                acc_ref[f, :] = acc_ref[f, :] * decay[:, q] + mixed[f, q]
+            acc_ref[...] = acc_ref[...] * decay + mixed
         return top, summed
 
-    last = nz // 2
-    ready = [(z, [(0, 0, 0), (0, 0, 1)])]
     state = None
-    for hop in range(1, last + 1):
-        coming = {}
-        for j in (0, 1):
-            for d in (0, 1):
-                if (d, hop, j) not in live:
-                    continue
-                src_z = zat(-hop if d == 0 else hop)
-                live[d, hop, j].wait_recv()
-                if hop + 1 < last or (hop + 1 == last and d == j):
-                    pass_on(src_z, j, d, hop + 1)
-                to_sib(src_z, j, d, hop)
-                coming.setdefault(d if hop < last else 0, (src_z, []))[1].append((d, hop, j))
-        for src_z, keys_ in ready:
-            for key in keys_:
-                sibs[key].wait_recv()
-            state = attend(src_z, state)
-        ready = list(coming.values())
-    for src_z, keys_ in ready:
-        for key in keys_:
-            sibs[key].wait_recv()
-        state = attend(src_z, state)
-
-    total_w = state[1]
-    att = []
-    for i in range(heads):
-        f, q = slice(i * HEAD_DIM, (i + 1) * HEAD_DIM), slice(i * rows, (i + 1) * rows)
-        att.append((acc_ref[f, :] / total_w[:, q]).astype(BF).astype(F32))
-    att = jnp.concatenate(att, axis=0)
-    ob = hw // 128
-    att_st = jnp.concatenate(
-        [jnp.transpose(att[cb * 128 : (cb + 1) * 128]) for cb in range(ob)], axis=0
-    ).astype(BF)
-
-    n2 = peers * 2 * ob
-    ob_bits = {1: 0, 2: 1}[ob]
-    tall, tall1 = iota((n2, peers), 0), iota((n2, peers), 1)
-    picked = None
-    for k in range(2):
-        e2 = onehot(((tall >> (ob_bits + 1)) == tall1) & (((tall >> ob_bits) & 1) == k))
-        part = mm(e2, place_u[k])
-        picked = part if picked is None else picked + part
-    lowbit = iota((n2, rows), 0) & (ob - 1)
-    a3 = jnp.concatenate([jnp.where(lowbit == cb, picked, 0.0) for cb in range(ob)], axis=1).astype(BF)
-    sb2[...] = mm(a3, att_st).reshape(peers, 2 * ob, 128).astype(BF)
+    ready = [0]
+    for d in near:
+        kv_live[d].wait_recv()
+        to_sib(d)
+        if len(ready) > 1 or d == near[0]:
+            first = ready.pop(0)
+            sibs[first].wait_recv()
+            state = attend(zat(-first), state)
+        ready.append(d)
+    for d in ready:
+        sibs[d].wait_recv()
+        state = attend(zat(-d), state)
+
+    att = (acc_ref[...] / state[1]).astype(BF).astype(F32)
+    zeros = jnp.zeros_like(att)
+    sent = mm(back_ref[0], jnp.transpose(jnp.concatenate([att, zeros], axis=0)).astype(BF))
+    sent = sent + mm(back_ref[1], jnp.transpose(jnp.concatenate([zeros, att], axis=0)).astype(BF))
+    sb2[...] = sent.reshape(peers, 4, 128).astype(BF)
 
     def send_back(k, carry):
         t = lax.rem(me + k, peers)
@@ -392,13 +418,19 @@
         part = mm(pick_g, piece.astype(BF))
         gate = part if gate is None else gate + part
 
-    code2 = t_col * (2 * ob) + rank_col * ob
     drain(rb2.at[pl.ds(0, peers - 1)], b_r)
     back = rb2[...].astype(F32).reshape(n2, 128).astype(BF)
     wide2 = iota((rows, n2), 1)
+    code2 = (t_col >> 4) * 64 + (t_col & 15)
     code2 = jnp.concatenate([code2] * (n2 // rows), axis=1)
-    for cb in range(ob):
-        og[h, :, cb * 128 : (cb + 1) * 128] = mm(onehot(wide2 == code2 + cb), back).astype(BF)
+    low = iota((rows, 128), 1) < HEAD_DIM
+    as_is = low == (rank_col == 0)
+    for cb in range(heads // 2):
+        first = mm(onehot(wide2 == code2 + 16 * (2 * cb)), back)
+        second = mm(onehot(wide2 == code2 + 16 * (2 * cb + 1)), back)
+        both = jnp.where(low, first, second)
+        swapped = pltpu.roll(jnp.where(low, second, first), HEAD_DIM, 1)
+        og[h, :, cb * 128 : (cb + 1) * 128] = jnp.where(as_is, both, swapped).astype(BF)
     os_ = []
     for k in (2, 1, 3) if nh == 4 else range(1, nh):
         cp = remote(og.at[h], og.at[h], o_s.at[k], o_r.at[k], head=lax.rem(h + k, nh))
@@ -412,10 +444,17 @@
     for i in range(nh):
         part = mm(og[i], wo_all[i])
         projected = part if projected is None else projected + part
-    out_ref[...] = (lat_ref[...].astype(F32) + gate * projected).astype(BF)
-
-    for c in os_ + wo_fwd + wo_sends + sends + list(sibs.values()):
+    out_ref[...] = gate * projected
+
+    for c in os_ + wo_fwd + wo_sends + list(kv_live.values()) + list(sibs.values()):
         c.wait_send()
+    for i in range(heads):
+        to, cp = q_copy(i)
+
+        @pl.when(to != s)
+        def _():
+            cp.wait_send()
+
     drain(rtab.at[pl.ds(0, ns - 1)], rz_s)
     drain(rtab.at[pl.ds(0, (np_ - 1) * ns)], ry_s)
     drain(rb.at[pl.ds(0, peers - 1)], d_s)
@@ -428,29 +467,29 @@
     peers = np_ * ns
     blocks = cols // 128
     hw = qkv_weight.shape[2]
-    ob = hw // 128
     width = cols * nh
     vm = pl.BlockSpec(memory_space=pltpu.VMEM)
     hbm = pl.BlockSpec(memory_space=pl.ANY)
     D = pltpu.SemaphoreType.DMA
     V = pltpu.VMEM
-    return pl.pallas_call(
+    change = pl.pallas_call(
         functools.partial(kernel, np_, ns, nh),
-        out_shape=jax.ShapeDtypeStruct((rows, cols), BF),
-        in_specs=[vm, vm, pl.BlockSpec(memory_space=pltpu.SMEM), vm, hbm, hbm, hbm],
+        out_shape=jax.ShapeDtypeStruct((rows, cols), F32),
+        in_specs=[hbm] * 7,
         out_specs=vm,
         scratch_shapes=[
+            V((rows, cols), BF), V((1, rows), I32), pltpu.SMEM((1, 8), I32), V((2, HEAD_DIM), F32),
             V((peers, 2 * blocks, 128), BF), V((peers, 2 * blocks, 128), BF),
-            V((peers, 2 * ob, 128), BF), V((peers, 2 * ob, 128), BF),
+            V((peers, 4, 128), BF), V((peers, 4, 128), BF),
             V((peers, 1, 128), I32),
             V((nh, rows, cols), BF), V((nh, rows, hw), BF),
             V((8, 3 * width), F32), V((3, width, hw), BF), V((hw, width), BF), V((nh, hw, cols), BF),
             V((8, cols + 256), F32), V((np_, 8, cols + 256), F32),
-            V((ns, rows, hw), BF), V((ns, hw, rows), BF),
-            V((rows, width), F32), V((rows, width), F32), V((hw, rows), F32),
-            pltpu.SemaphoreType.REGULAR, D((3,)),
-            D, D, D, D, D, D, D((4,)), D((4,)), D((4,)), D((4,)), D((6,)), D((6,)), D, D,
-            D((2, 5, 2)), D((2, 5, 2)), D((2, 5, 2)), D((2, 5, 2)), D, D, D((4,)), D((4,)),
+            V((4, rows, 128), BF), V((ns, rows, 128), BF), V((4, HEAD_DIM, rows), BF), V((4, HEAD_DIM, rows), BF),
+            V((2, peers * 4, 4 * rows), BF), V((rows, width), F32), V((rows, width), F32), V((HEAD_DIM, 4 * rows), F32),
+            pltpu.SemaphoreType.REGULAR, D((7,)),
+            D, D, D, D, D, D, D((4,)), D((4,)), D((4,)), D((4,)), D((12,)), D((12,)), D, D,
+            D((8,)), D((8,)), D((8,)), D((8,)), D((4,)), D((4,)), D, D, D((4,)), D((4,)),
         ],
         compiler_params=pltpu.CompilerParams(
             collective_id=0, has_side_effects=True, vmem_limit_bytes=56 << 20
@@ -459,6 +498,7 @@
         latents, route.reshape(1, rows), seg_lengths, qk_gain, modulation[0],
         qkv_weight.transpose(1, 0, 2), out_weight,
     )
+    return (latents.astype(F32) + change).astype(BF)
 
 
 def solution(mesh):

time: 78.1 us -> 70.7 us (0.905)
  Pallas kernels: 76.3 us -> 69 us
  other arithmetic: 0 us -> 1.63 us
  local copies, waits for them, and re-layouts: 1.57 us -> 0.01 us
    pallas_call x1, Pallas kernels: 76.3 us -> 69 us  [local(): pl.pallas_call(functools.partial(kernel, np_, ns, nh), out_shape=jax.Shap...]
    convert_element_type x0 -> x1, other arithmetic: none -> 1.63 us  [local(): return (latents.astype(F32) + change).astype(BF)]
    unnamed x1 -> x2, local copies, waits for them, and re-layouts: 1.57 us -> 0.01 us
where the time goes in v2:
time: 70.7 us; the launch traced here: 70.6 us
  Pallas kernels  69 us (98%)
  other arithmetic  1.63 us (2%)
    pallas_call x1, Pallas kernels, local(): pl.pallas_call(functools.partial(kernel, np_, ns, nh), out_shape=jax.Shap...  69 us
    convert_element_type x1, other arithmetic, local(): return (latents.astype(F32) + change).astype(BF)  1.63 us

profile of v2, /device:TPU:1, one launch (start us, length us, event | category | flops | bytes accessed | tf_op | source)
XLA Modules:
  0.0 70.6 jit_solution(13452338496043505197)
XLA Ops:
  0.0 0.0 copy-start
  0.0 69.0 %shard_map.73 = f32[128,512]{1,0:T(8,128)} custom-call(bf16[128,512]{1,0:T(8,128)(2,1)} %lat_hbm.1, s32[1,128]{1,0:T(1,128)} %bitcast.5, s32[1,8]{1,0:T(1,128)} %len_hbm.1, f32[2,64]{1,0:T(2,128)} %gain_hbm.1, f32[8,6144]{1,0:T(8,128)} %bitcast.4, bf16[3,2048,256]{2,1,0:T(8,128)(2,1)} %bitcast.3, bf16[256,2048]{1,0:T(8,128)(2,1)} %wo_hbm.1), custom_call_target="tpu_custom_call" | custom-call | tf_op jit(solution)/shard_map/pallas_call | solution.py:475
  69.0 0.0 copy-done
  69.0 1.6 %add_convert_fusion = bf16[128,512]{1,0:T(8,128)(2,1)} fusion(f32[128,512]{1,0:T(8,128)} %shard_map.73, bf16[128,512]{1,0:T(8,128)(2,1)S(1)} %copy-done), kind=kLoop, calls=%fused_computation | loop fusion | flops 196608 | bytes 524288 | tf_op jit(solution)/shard_map/convert_element_type | solution.py:501
Async XLA Ops:
  0.0 69.0 %copy-start = (bf16[128,512]{1,0:T(8,128)(2,1)S(1)}, bf16[128,512]{1,0:T(8,128)(2,1)}, u32[]{:S(2)}) copy-start(bf16[128,512]{1,0:T(8,128)(2,1)} %lat_hbm.1) | copy-start | bytes 393220

commit v3 on v2

--- a/solution.py
+++ b/solution.py
@@ -257,8 +257,6 @@
 
     for c in to_right[2:] + to_left[2:] + onward:
         c.wait_recv()
-    for c in to_right + to_left + onward:
-        c.wait_send()
 
     feats = jnp.concatenate([xbuf[i] for i in range(nh)], axis=1).astype(F32)
     centred = feats - jnp.mean(feats, axis=1, keepdims=True)
@@ -277,6 +275,25 @@
         return (v * lax.rsqrt(mean_sq + EPS) * gain).astype(BF)
 
     gains = jnp.concatenate([gain_ref[...]] * heads, axis=1)
+    query = rms(mm(normed, wv[0]), gains[0:1])
+    q_send[...] = jnp.transpose(query.astype(F32) * 0.125).astype(BF).reshape(heads, HEAD_DIM, rows)
+    quarter, part_of = s // 4, lax.rem(s, 4)
+
+    def q_copy(i):
+        to = i * 4 + quarter
+        return to, remote(q_send.at[i], q_buf.at[part_of], q_s.at[i], q_r.at[part_of], seq=to)
+
+    for i in range(heads):
+        to, cp = q_copy(i)
+
+        @pl.when(to != s)
+        def _():
+            cp.start()
+
+        @pl.when(to == s)
+        def _():
+            q_buf[part_of] = q_send[i]
+
     keys = rms(mm(normed, wv[1]), gains[1:2])
     vals = mm(normed, wv[2]).astype(BF)
     from_lane, to_lane = iota((hw, 2 * hw), 0), iota((hw, 2 * hw), 1)
@@ -293,7 +310,8 @@
     for d in range(1, nz // 2 + 1):
         near += [d, nz - d] if 2 * d < nz else [d]
     kv_live, sibs = {}, {}
-    for d in reversed(near):
+    near = near[::-1]
+    for d in near:
         to = zat(d)
         kv_live[d] = remote(kv_send.at[to // 2], kv_buf.at[s], k_s.at[d], k_r.at[d], seq=to * 2 + core)
         kv_live[d].start()
@@ -305,25 +323,6 @@
 
     kv_buf[s] = kv_send[my_head]
     to_sib(0)
-
-    query = rms(mm(normed, wv[0]), gains[0:1])
-    q_send[...] = jnp.transpose(query.astype(F32) * 0.125).astype(BF).reshape(heads, HEAD_DIM, rows)
-    quarter, part_of = s // 4, lax.rem(s, 4)
-
-    def q_copy(i):
-        to = i * 4 + quarter
-        return to, remote(q_send.at[i], q_buf.at[part_of], q_s.at[i], q_r.at[part_of], seq=to)
-
-    for i in range(heads):
-        to, cp = q_copy(i)
-
-        @pl.when(to != s)
-        def _():
-            cp.start()
-
-        @pl.when(to == s)
-        def _():
-            q_buf[part_of] = q_send[i]
 
     n2 = peers * 4
     tall, tall1 = iota((n2, peers), 0), iota((n2, peers), 1)
@@ -431,22 +430,20 @@
         both = jnp.where(low, first, second)
         swapped = pltpu.roll(jnp.where(low, second, first), HEAD_DIM, 1)
         og[h, :, cb * 128 : (cb + 1) * 128] = jnp.where(as_is, both, swapped).astype(BF)
-    os_ = []
+    from_head = {}
     for k in (2, 1, 3) if nh == 4 else range(1, nh):
-        cp = remote(og.at[h], og.at[h], o_s.at[k], o_r.at[k], head=lax.rem(h + k, nh))
-        cp.start()
-        os_.append(cp)
+        from_head[k] = remote(og.at[h], og.at[h], o_s.at[k], o_r.at[k], head=lax.rem(h + k, nh))
+        from_head[k].start()
     for c in wo_fwd:
         c.wait_recv()
-    for c in os_:
-        c.wait_recv()
-    projected = None
-    for i in range(nh):
-        part = mm(og[i], wo_all[i])
-        projected = part if projected is None else projected + part
-    out_ref[...] = gate * projected
-
-    for c in os_ + wo_fwd + wo_sends + list(kv_live.values()) + list(sibs.values()):
+    projected = mm(og[h], wo_all[h])
+    for k in (1, 3, 2) if nh == 4 else range(1, nh):
+        source = lax.rem(h + nh - k, nh)
+        from_head[k].wait_recv()
+        projected = projected + mm(og[source], wo_all[source])
+    out_ref[...] = (lat_ref[...].astype(F32) + gate * projected).astype(BF)
+
+    for c in to_right + to_left + onward + list(from_head.values()) + wo_fwd + wo_sends + list(kv_live.values()) + list(sibs.values()):
         c.wait_send()
     for i in range(heads):
         to, cp = q_copy(i)
@@ -474,7 +471,7 @@
     V = pltpu.VMEM
     change = pl.pallas_call(
         functools.partial(kernel, np_, ns, nh),
-        out_shape=jax.ShapeDtypeStruct((rows, cols), F32),
+        out_shape=pltpu.VMEM((rows, cols), BF),
         in_specs=[hbm] * 7,
         out_specs=vm,
         scratch_shapes=[
@@ -498,7 +495,7 @@
         latents, route.reshape(1, rows), seg_lengths, qk_gain, modulation[0],
         qkv_weight.transpose(1, 0, 2), out_weight,
     )
-    return (latents.astype(F32) + change).astype(BF)
+    return change
 
 
 def solution(mesh):

time: 70.7 us -> 67.4 us (0.953)
  Pallas kernels: 69 us -> 66.6 us
  other arithmetic: 1.63 us -> 0 us
    pallas_call x1, Pallas kernels: 69 us -> 66.6 us  [local(): pl.pallas_call(functools.partial(kernel, np_, ns, nh), out_shape=pltpu.VM...]
    convert_element_type x1 -> x0, other arithmetic: 1.63 us -> none  [local(): return (latents.astype(F32) + change).astype(BF)]
where the time goes in v3:
time: 67.4 us; the launch traced here: 67.3 us
  Pallas kernels  66.6 us (99%)
    pallas_call x1, Pallas kernels, local(): pl.pallas_call(functools.partial(kernel, np_, ns, nh), out_shape=pltpu.VM...  66.6 us

profile of v3, /device:TPU:1, one launch (start us, length us, event | category | flops | bytes accessed | tf_op | source)
XLA Modules:
  0.0 67.3 jit_solution(17159044661383219722)
XLA Ops:
  0.0 66.6 %shard_map.73 = bf16[128,512]{1,0:T(8,128)(2,1)S(1)} custom-call(bf16[128,512]{1,0:T(8,128)(2,1)} %lat_hbm.1, s32[1,128]{1,0:T(1,128)} %bitcast.5, s32[1,8]{1,0:T(1,128)} %len_hbm.1, f32[2,64]{1,0:T(2,128)} %gain_hbm.1, f32[8,6144]{1,0:T(8,128)} %bitcast.4, bf16[3,2048,256]{2,1,0:T(8,128)(2,1)} %bitcast.3, bf16[256,2048]{1,0:T(8,128)(2,1)} %wo_hbm.1), custom_call_target="tpu_custom_call" | custom-call | tf_op jit(solution)/shard_map/pallas_call | solution.py:472
  66.6 0.7 copy.9

commit v4 on v3

--- a/solution.py
+++ b/solution.py
@@ -141,6 +141,11 @@
 
     lax.fori_loop(0, (ns - 1) * (np_ - 1), send_rows, 0)
 
+    drain(rtab.at[pl.ds(0, ns - 1)], rz_r)
+    own_line = rtab.at[pl.ds(pl.multiple_of(p * ns, ns), ns)]
+    for k in range(1, np_):
+        remote(own_line, own_line, ry_s, ry_r, pool=lax.rem(p + k, np_)).start()
+
     loads[2].wait()
     half = wov.shape[0] // 2
     mine = pl.ds(pl.multiple_of(core * half, half), half)
@@ -155,11 +160,6 @@
         cp.start()
         wo_sends.append(cp)
     wo_all[h] = wov[:, pl.ds(pl.multiple_of(h * cols, cols), cols)]
-
-    drain(rtab.at[pl.ds(0, ns - 1)], rz_r)
-    own_line = rtab.at[pl.ds(pl.multiple_of(p * ns, ns), ns)]
-    for k in range(1, np_):
-        remote(own_line, own_line, ry_s, ry_r, pool=lax.rem(p + k, np_)).start()
 
     first[2].wait()
     first[3].wait()

time: 67.4 us -> 67.2 us (level)
  no operation moved by 1% of the time
where the time goes in v4:
time: 67.2 us; the launch traced here: 67.1 us
  Pallas kernels  66.4 us (99%)
    pallas_call x1, Pallas kernels, local(): pl.pallas_call(functools.partial(kernel, np_, ns, nh), out_shape=pltpu.VM...  66.4 us

profile of v4, /device:TPU:1, one launch (start us, length us, event | category | flops | bytes accessed | tf_op | source)
XLA Modules:
  0.0 67.1 jit_solution(9418101757014783782)
XLA Ops:
  0.0 66.4 %shard_map.73 = bf16[128,512]{1,0:T(8,128)(2,1)S(1)} custom-call(bf16[128,512]{1,0:T(8,128)(2,1)} %lat_hbm.1, s32[1,128]{1,0:T(1,128)} %bitcast.5, s32[1,8]{1,0:T(1,128)} %len_hbm.1, f32[2,64]{1,0:T(2,128)} %gain_hbm.1, f32[8,6144]{1,0:T(8,128)} %bitcast.4, bf16[3,2048,256]{2,1,0:T(8,128)(2,1)} %bitcast.3, bf16[256,2048]{1,0:T(8,128)(2,1)} %wo_hbm.1), custom_call_target="tpu_custom_call" | custom-call | tf_op jit(solution)/shard_map/pallas_call | solution.py:472
  66.4 0.7 copy.9
